TPU v7x, 32 devices: a whole 2x2x4 slice. The times are simulated.
32 devices in a mesh: chan: 4 (over y, x), tile: 8 (over z, core).
Axes of the slice: x: 2, y: 2, z: 4, core: 2. Of those that a mesh axis runs over, the one named last changes fastest.
Arguments:
- pixels: bfloat16 [32, 256, 1024], P('tile', None, 'chan'), may hold values from -6 to 6
- conv_weight: bfloat16 [3, 3, 1024, 1024], P(None, None, 'tile', 'chan'), may hold values from -0.0625 to 0.0625
- conv_bias: float32 [1024], P('chan'), may hold values from -3 to 3
- depth_weight: float32 [7, 7, 1024], P(None, None, 'chan'), may hold values from -0.875 to 0.875
- depth_bias: float32 [1024], P('chan'), may hold values from -3 to 3
Outputs:
- features: bfloat16 [32, 256, 1024], P('tile', None, 'chan')
All inputs are finite; a program needn't handle non-finite values.
Results may differ from a plain program's by a relative error of at most 0.0043.
Values may be sent and summed in bfloat16 or wider, within the bound.
A program may use at most 64 MiB of HBM per device.

v0:
```python
import jax
import jax.numpy as jnp
from jax import lax
from jax.sharding import PartitionSpec as P


def padded_2(block, sides, width):
    for axis, dim in sides:
        count = lax.axis_size(axis)
        forward = [(i, i + 1) for i in range(count - 1)]
        backward = [(target, source) for source, target in forward]
        low = lax.ppermute(
            lax.slice_in_dim(block, block.shape[dim] - width, None, axis=dim), axis, forward
        )
        high = lax.ppermute(lax.slice_in_dim(block, 0, width, axis=dim), axis, backward)
        block = jnp.concatenate([low, block, high], axis=dim)
    return block


def tap_sum(running, padded, filters, out_rows, image_cols):
    block_width = padded.shape[2]
    for row_off in range(3):
        for col_off in range(3):
            window = padded[
                row_off : row_off + out_rows, col_off : col_off + image_cols, :
            ].reshape(out_rows * image_cols, block_width)
            running = running + jnp.dot(
                window, filters[row_off, col_off], preferred_element_type=jnp.float32
            )
    return running


def body(pixels, conv_weight, conv_bias, depth_weight, depth_bias):
    tile_rows, image_cols, own_channels = pixels.shape
    gathered = lax.all_gather(conv_weight, "tile", axis=2, tiled=True)
    extent = 1
    out_rows = tile_rows + 2 * (extent - 1)
    count_pixels = out_rows * image_cols
    rimmed = padded_2(pixels, (("tile", 0),), extent)
    padded = jnp.pad(rimmed, ((0, 0), (1, 1), (0, 0)))
    initial = jnp.zeros((count_pixels, own_channels), jnp.float32)
    convolved = tap_sum(
        initial, lax.all_gather(padded, "chan", axis=2, tiled=True), gathered, out_rows, image_cols
    )
    convolved = convolved.reshape(out_rows, image_cols, own_channels)
    hidden = jax.nn.relu(convolved + conv_bias).astype(jnp.bfloat16)
    widened = padded_2(hidden, (("tile", 0),), 3)
    spread = jnp.pad(widened, ((0, 0), (3, 3), (0, 0))).astype(jnp.float32)
    running = jnp.zeros((tile_rows, image_cols, own_channels), jnp.float32)
    for row_off in range(7):
        for col_off in range(7):
            running = (
                running
                + spread[row_off : row_off + tile_rows, col_off : col_off + image_cols, :]
                * depth_weight[row_off, col_off]
            )
    return (running + depth_bias).astype(jnp.bfloat16)


def solution(mesh):
    in_specs = (
        P("tile", None, "chan"),
        P(None, None, "tile", "chan"),
        P("chan"),
        P(None, None, "chan"),
        P("chan"),
    )
    out_specs = P("tile", None, "chan")
    return jax.shard_map(body, mesh=mesh, in_specs=in_specs, out_specs=out_specs, check_vma=False)
```

profile of v0, /device:TPU:1, one launch (start us, length us, event | category | flops | bytes accessed | tf_op | source)
XLA Modules:
  0.0 160.2 jit_solution(10032444558347180040)
XLA Ops:
  6.5 0.0 copy-start.8
  6.5 0.0 all-gather.3.cloned.1.call-start
  6.5 1.0 fusion.66
  7.5 4.6 %collective-permute-start = (bf16[1,256,256]{2,1,0:T(8,128)(2,1)S(1)}, bf16[1,256,256]{2,1,0:T(8,128)(2,1)S(1)}, u32[]{:S(2)}, u32[]{:S(2)}) collective-permute-start(bf16[1,256,256]{2,1,0:T(8,128)(2,1)S(1)} %get-tuple-element.16), channel_id=1, source_target_pairs={{0,1},{1,2},{2,3},{3,4},{4,5},{5,6},{6,7},{8,9},{9,10},{10,11},{11... | collective-permute-start | bytes 393224 | tf_op jit(solution)/shard_map/ppermute | solution.py:12
  12.1 1.9 %collective-permute-start.1 = (bf16[1,256,256]{2,1,0:T(8,128)(2,1)S(1)}, bf16[1,256,256]{2,1,0:T(8,128)(2,1)S(1)}, u32[]{:S(2)}, u32[]{:S(2)}) collective-permute-start(bf16[1,256,256]{2,1,0:T(8,128)(2,1)S(1)} %get-tuple-element.17), channel_id=1, source_target_pairs={{1,0},{2,1},{3,2},{4,3},{5,4},{6,5},{7,6},{9,8},{10,9},{11,10},{12... | collective-permute-start | bytes 393224 | tf_op jit(solution)/shard_map/ppermute | solution.py:15
  14.1 0.0 collective-permute-done
  14.1 4.3 %collective-permute-done.1 = bf16[1,256,256]{2,1,0:T(8,128)(2,1)S(1)} collective-permute-done((bf16[1,256,256]{2,1,0:T(8,128)(2,1)S(1)}, bf16[1,256,256]{2,1,0:T(8,128)(2,1)S(1)}, u32[]{:S(2)}, u32[]{:S(2)}) %collective-permute-start.1) | collective-permute-done | bytes 131104 | tf_op jit(solution)/shard_map/ppermute | solution.py:15
  18.4 2.2 %fusion.62 = bf16[6,258,256]{2,1,0:T(8,128)(2,1)} fusion(bf16[1,256,256]{2,1,0:T(8,128)(2,1)S(1)} %collective-permute-done.1, bf16[4,256,256]{2,1,0:T(8,128)(2,1)} %param.5, bf16[1,256,256]{2,1,0:T(8,128)(2,1)S(1)} %collective-permute-done), kind=kLoop, calls=%fused_computation.124 | loop fusion | flops 4755456 | bytes 1579008 | tf_op jit(solution)/shard_map/concatenate | solution.py:16
  20.6 0.0 all-gather.3.cloned.1.call-update
  20.6 0.0 all-gather.5.cloned.1.call-start
  20.7 0.7 all-gather.5.cloned.1.call-update
  21.4 0.0 copy-done.8
  21.4 43.7 %all-gather.3.cloned.1.call-done = bf16[6,258,1024]{2,1,0:T(8,128)(2,1)} async-done(((bf16[6,258,256]{2,1,0:T(8,128)(2,1)}), bf16[6,258,1024]{2,1,0:T(8,128)(2,1)}) %all-gather.3.cloned.1.call-update) | async-done | bytes 3170320 | tf_op jit(solution)/shard_map/all_gather | solution.py:43
  65.2 14.1 %fusion.64 = (bf16[4,256,1024]{2,1,0:T(8,128)(2,1)S(1)}, bf16[4,256,1024]{2,1,0:T(8,128)(2,1)}, bf16[4,256,1024]{2,1,0:T(8,128)(2,1)}, bf16[4,256,1024]{2,1,0:T(...) fusion(bf16[6,258,1024]{2,1,0:T(8,128)(2,1)} %all-gather.3.clon, ...), kind=kLoop, calls=%fused_computation.135 | loop fusion | bytes 37748736 | tf_op jit(solution)/shard_map/slice | solution.py:24
  79.3 39.6 %all-gather.5.cloned.1.call-done = bf16[3,3,1024,256]{3,2,1,0:T(8,128)(2,1)} async-done(((bf16[3,3,128,256]{3,2,1,0:T(8,128)(2,1)}), bf16[3,3,1024,256]{3,2,1,0:T(8,128)(2,1)}) %all-gather.5.cloned.1.call-update) | async-done | bytes 4718608 | tf_op jit(solution)/shard_map/all_gather | solution.py:35
  118.9 0.0 copy-start.6
  118.9 2.5 %fusion.63 = f32[1024,256]{1,0:T(8,128)S(1)} fusion(bf16[1024,1024]{1,0:T(8,128)(2,1)} %bitcast.104, bf16[3,3,1024,256]{3,2,1,0:T(8,128)(2,1)} %all-gather.5.cloned.1.call-done), kind=kOutput, calls=%fused_computation.134 | convolution fusion | flops 536870912 | bytes 3670016 | tf_op jit(solution)/shard_map/dot_general | solution.py:27
  121.4 0.0 copy-done.6
  121.4 0.0 copy-start.5
  121.4 0.0 copy-start.7
  121.4 1.9 %convolution_add_fusion.7 = f32[1024,256]{1,0:T(8,128)S(1)} fusion(f32[1024,256]{1,0:T(8,128)S(1)} %fusion.63, bf16[1024,1024]{1,0:T(8,128)(2,1)S(1)} %bitcast.102, bf16[3,3,1024,256]{3,2,1,0:T(8,128)(2,1)} %all-gather.5.cloned.1.call-done), kind=kOutput, calls=%fused_computation.16 | convolution fusion | flops 537133056 | bytes 4718592 | tf_op jit(solution)/shard_map/dot_general | solution.py:27
  123.4 0.0 copy-done.5
  123.4 1.2 copy-done.7
  124.6 0.0 copy-start.4
  124.6 0.7 convolution_add_fusion.6
  125.3 0.9 copy-done.4
  126.2 0.0 copy-start.3
  126.2 0.7 convolution_add_fusion.5
  126.9 0.9 copy-done.3
  127.8 0.0 copy-start.2
  127.8 0.7 convolution_add_fusion.4
  128.5 0.9 copy-done.2
  129.3 0.0 copy-start.1
  129.3 0.7 convolution_add_fusion.3
  130.1 0.9 copy-done.1
  130.9 0.0 copy-start
  130.9 0.7 convolution_add_fusion.2
  131.6 0.9 copy-done
  132.5 0.7 convolution_add_fusion.1
  133.2 0.0 copy-start.10
  133.3 0.7 convolution_add_fusion
  134.0 0.0 copy-done.10
  134.0 0.1 maximum_convert_fusion
  134.1 0.1 fusion.65
  134.2 1.9 %collective-permute-start.2 = (bf16[3,256,256]{2,1,0:T(8,128)(2,1)S(1)}, bf16[3,256,256]{2,1,0:T(8,128)(2,1)S(1)}, u32[]{:S(2)}, u32[]{:S(2)}) collective-permute-start(bf16[3,256,256]{2,1,0:T(8,128)(2,1)S(1)} %get-tuple-element.14), channel_id=1, source_target_pairs={{0,1},{1,2},{2,3},{3,4},{4,5},{5,6},{6,7},{8,9},{9,10},{10,11},{11... | collective-permute-start | bytes 1179656 | tf_op jit(solution)/shard_map/ppermute | solution.py:12
  136.1 2.4 %collective-permute-start.3 = (bf16[3,256,256]{2,1,0:T(8,128)(2,1)S(1)}, bf16[3,256,256]{2,1,0:T(8,128)(2,1)S(1)}, u32[]{:S(2)}, u32[]{:S(2)}) collective-permute-start(bf16[3,256,256]{2,1,0:T(8,128)(2,1)S(1)} %get-tuple-element.15), channel_id=1, source_target_pairs={{1,0},{2,1},{3,2},{4,3},{5,4},{6,5},{7,6},{9,8},{10,9},{11,10},{12... | collective-permute-start | bytes 1179656 | tf_op jit(solution)/shard_map/ppermute | solution.py:15
  138.6 0.0 copy-start.9
  138.6 2.2 %collective-permute-done.2 = bf16[3,256,256]{2,1,0:T(8,128)(2,1)S(1)} collective-permute-done((bf16[3,256,256]{2,1,0:T(8,128)(2,1)S(1)}, bf16[3,256,256]{2,1,0:T(8,128)(2,1)S(1)}, u32[]{:S(2)}, u32[]{:S(2)}) %collective-permute-start.2) | collective-permute-done | bytes 393248 | tf_op jit(solution)/shard_map/ppermute | solution.py:12
  140.8 4.4 %collective-permute-done.3 = bf16[3,256,256]{2,1,0:T(8,128)(2,1)S(1)} collective-permute-done((bf16[3,256,256]{2,1,0:T(8,128)(2,1)S(1)}, bf16[3,256,256]{2,1,0:T(8,128)(2,1)S(1)}, u32[]{:S(2)}, u32[]{:S(2)}) %collective-permute-start.3) | collective-permute-done | bytes 393248 | tf_op jit(solution)/shard_map/ppermute | solution.py:15
  145.2 0.3 fusion.7
  145.5 0.0 copy-done.9
  145.5 7.9 %fusion.10 = bf16[4,256,256]{2,1,0:T(8,128)(2,1)} fusion(f32[10,262,256]{2,1,0:T(8,128)S(1)} %fusion.7, f32[256]{0:T(256)S(1)} %copy-done.9, f32[256]{0:T(256)S(1)} %bitcast.133, f32[256]{0:T(256)S(1)} %bitcast.134, f32[256]{0:T(256)S(1)} %bitcast.106, f32[256]{0:T(256)S(1)} %bitcast.107, f32[256]{0:T(256)S(1)} %bitcast.108, f32[256]{0:T(256)S(1)} %bitcast.109, ...), kind=kLoop, calls=%fused_computation.23 | loop fusion | flops 25952256 | bytes 51955712 | tf_op jit(solution)/shard_map/convert_element_type | solution.py:57
  (3 shorter events, 0.1 us)
Async XLA Ops:
  6.5 14.9 %copy-start.8 = (f32[7,7,256]{2,1,0:T(8,128)S(1)}, f32[7,7,256]{2,1,0:T(8,128)}, u32[]{:S(2)}) copy-start(f32[7,7,256]{2,1,0:T(8,128)} %param.8) | copy-start | bytes 150532
  6.5 58.6 %all-gather.3.cloned.1.call-start = ((), (), s32[]{:S(2)}) async-start(), calls=%async_computation | async-start | bytes 4055040 | tf_op jit(solution)/shard_map/all_gather | solution.py:43
  7.5 6.5 %collective-permute-start = (bf16[1,256,256]{2,1,0:T(8,128)(2,1)S(1)}, bf16[1,256,256]{2,1,0:T(8,128)(2,1)S(1)}, u32[]{:S(2)}, u32[]{:S(2)}) collective-permute-start(bf16[1,256,256]{2,1,0:T(8,128)(2,1)S(1)} %get-tuple-element.16), channel_id=1, source_target_pairs={{0,1},{1,2},{2,3},{3,4},{4,5},{5,6},{6,7},{8,9},{9,10},{10,11},{11... | collective-permute-start | bytes 393224 | tf_op jit(solution)/shard_map/ppermute | solution.py:12
  12.1 6.3 %collective-permute-start.1 = (bf16[1,256,256]{2,1,0:T(8,128)(2,1)S(1)}, bf16[1,256,256]{2,1,0:T(8,128)(2,1)S(1)}, u32[]{:S(2)}, u32[]{:S(2)}) collective-permute-start(bf16[1,256,256]{2,1,0:T(8,128)(2,1)S(1)} %get-tuple-element.17), channel_id=1, source_target_pairs={{1,0},{2,1},{3,2},{4,3},{5,4},{6,5},{7,6},{9,8},{10,9},{11,10},{12... | collective-permute-start | bytes 393224 | tf_op jit(solution)/shard_map/ppermute | solution.py:15
  20.6 98.2 %all-gather.5.cloned.1.call-start = ((), (), s32[]{:S(2)}) async-start(), calls=%async_computation.1 | async-start | bytes 5308416 | tf_op jit(solution)/shard_map/all_gather | solution.py:35
  118.9 2.5 %copy-start.6 = (bf16[4,256,1024]{2,1,0:T(8,128)(2,1)S(1)}, bf16[4,256,1024]{2,1,0:T(8,128)(2,1)}, u32[]{:S(2)}) copy-start(bf16[4,256,1024]{2,1,0:T(8,128)(2,1)} %get-tuple-element.12) | copy-start | bytes 6291460
  121.4 1.9 %copy-start.5 = (bf16[4,256,1024]{2,1,0:T(8,128)(2,1)S(1)}, bf16[4,256,1024]{2,1,0:T(8,128)(2,1)}, u32[]{:S(2)}) copy-start(bf16[4,256,1024]{2,1,0:T(8,128)(2,1)} %get-tuple-element.11) | copy-start | bytes 6291460
  121.4 3.1 %copy-start.7 = (bf16[3,3,1024,256]{3,2,1,0:T(8,128)(2,1)S(1)}, bf16[3,3,1024,256]{3,2,1,0:T(8,128)(2,1)}, u32[]{:S(2)}) copy-start(bf16[3,3,1024,256]{3,2,1,0:T(8,128)(2,1)} %all-gather.5.cloned.1.call-done) | copy-start | bytes 14155780
  124.6 1.6 copy-start.4
  126.2 1.6 copy-start.3
  127.8 1.6 copy-start.2
  129.3 1.6 copy-start.1
  130.9 1.6 copy-start
  133.2 0.7 copy-start.10
  134.2 6.6 %collective-permute-start.2 = (bf16[3,256,256]{2,1,0:T(8,128)(2,1)S(1)}, bf16[3,256,256]{2,1,0:T(8,128)(2,1)S(1)}, u32[]{:S(2)}, u32[]{:S(2)}) collective-permute-start(bf16[3,256,256]{2,1,0:T(8,128)(2,1)S(1)} %get-tuple-element.14), channel_id=1, source_target_pairs={{0,1},{1,2},{2,3},{3,4},{4,5},{5,6},{6,7},{8,9},{9,10},{10,11},{11... | collective-permute-start | bytes 1179656 | tf_op jit(solution)/shard_map/ppermute | solution.py:12
  136.1 9.1 %collective-permute-start.3 = (bf16[3,256,256]{2,1,0:T(8,128)(2,1)S(1)}, bf16[3,256,256]{2,1,0:T(8,128)(2,1)S(1)}, u32[]{:S(2)}, u32[]{:S(2)}) collective-permute-start(bf16[3,256,256]{2,1,0:T(8,128)(2,1)S(1)} %get-tuple-element.15), channel_id=1, source_target_pairs={{1,0},{2,1},{3,2},{4,3},{5,4},{6,5},{7,6},{9,8},{10,9},{11,10},{12... | collective-permute-start | bytes 1179656 | tf_op jit(solution)/shard_map/ppermute | solution.py:15
  138.6 6.9 %copy-start.9 = (f32[256]{0:T(256)S(1)}, f32[256]{0:T(256)}, u32[]{:S(2)}) copy-start(f32[256]{0:T(256)} %param.9) | copy-start | bytes 3076
Sparse Core Ops, SparseCore 0:
  20.8 44.3 all-gather.2
  66.8 52.0 all-gather.4
where the time goes:
time: 161 us; the launch traced here: 160 us
  waiting for transfers between devices  95 us (59%)
  local copies, waits for them, and re-layouts  20.8 us (13%)
  between operations  13.6 us (8%)
  starting transfers between devices  10.9 us (7%)
  other arithmetic  10.5 us (7%)
  matrix products  9.39 us (6%)
    all_gather x1, waiting for transfers between devices, body(): lax.all_gather(padded, 'chan', axis=2, tiled=True)  43.7 us
    all_gather x1, waiting for transfers between devices, body(): gathered = lax.all_gather(conv_weight, 'tile', axis=2, tiled=True)  39.6 us
    slice x1, local copies, waits for them, and re-layouts, tap_sum(): padded[row_off:row_off + out_rows, col_off:col_off + image_cols, :]  14.1 us
    dot_general x9, matrix products, tap_sum(): jnp.dot(window, filters[row_off, col_off], preferred_element_type=jnp.flo...  9.39 us
    ppermute x2, waiting for transfers between devices, padded_2(): lax.ppermute(lax.slice_in_dim(block, 0, width, axis=dim), axis, backward)  8.74 us
    convert_element_type x1, other arithmetic, body(): return (running + depth_bias).astype(jnp.bfloat16)  7.92 us
    ppermute x2, starting transfers between devices, padded_2(): lax.ppermute(lax.slice_in_dim(block, block.shape[dim] - width, None, axis...  6.52 us
    unnamed x22, local copies, waits for them, and re-layouts  5.61 us
  transfers between devices with their start and end apart: 6, of which 5 were waited for; matrix products, arithmetic and copies ran while one was open for 9% of the time, Pallas kernels for 0%

commit v1 on v0

v1 whole, which is shorter than its diff:
```python
import functools

import jax
import jax.numpy as jnp
from jax import lax
from jax.experimental import pallas as pl
from jax.experimental.pallas import tpu as pltpu
from jax.sharding import PartitionSpec as P

PAD = 8
RIGHT, LEFT, SIBLING = 0, 1, 2


def kernel(
    chans, tiles, px_in, w_in, conv_bias, depth_weight, depth_bias, out,
    px, wt, acc, hid, hid_low, hid_high, spread, total, result,
    load_sem, w_recv, w_send, z_send, z_recv, p_recv, p_own, p_fwd_a, p_fwd_b,
    h_send, h_recv, out_sem,
):
    rows, cols, own = px_in.shape
    halves, _, _, depth, _ = wt.shape
    width = own // halves
    chips = tiles // 2
    per_unit = own // (2 * depth)
    units = chans
    high_count = chans // 2
    mid = rows // 2

    c, t = lax.axis_index("chan"), lax.axis_index("tile")
    q, core = t // 2, lax.rem(t, 2)
    other = 1 - core
    sibling = 2 * q + other
    partner = c + 1 - 2 * lax.rem(c, 2)
    peers = [lax.rem(c + 2 * j, chans) for j in range(1, high_count)]
    corners = [lax.rem(partner + 2 * j, chans) for j in range(1, high_count)]

    def remote(src, dst, send, recv, chan, tile):
        return pltpu.make_async_remote_copy(
            src_ref=src, dst_ref=dst, send_sem=send, recv_sem=recv,
            device_id=(chan, tile), device_id_type=pl.DeviceIdType.MESH,
        )

    def wait_for(ref, sem):
        pltpu.make_async_copy(ref, ref, sem).wait()

    barrier = pltpu.get_barrier_semaphore()

    def tell(chan, tile):
        pl.semaphore_signal(
            barrier, inc=1, device_id=(chan, tile), device_id_type=pl.DeviceIdType.MESH
        )

    shard = 2 * q + core
    loads = []
    for h in range(halves):
        for a in range(3):
            for b in range(3):
                loads.append(pltpu.make_async_copy(
                    w_in.at[a, b, :, pl.ds(h * width, width)],
                    wt.at[h, shard, a, :, pl.ds(b * width, width)],
                    load_sem.at[h, 3 * a + b],
                ))
    own_px = pltpu.make_async_copy(px_in, px.at[c, pl.ds(1, rows)], load_sem.at[halves, 0])
    for load in loads:
        load.start()
    own_px.start()

    near = (-2, -1, 1, 2)
    for step in near:
        @pl.when((t + step >= 0) & (t + step < tiles))
        def _():
            tell(c, t + step)
    for chan in [partner] + peers:
        tell(chan, t)
    count = high_count
    for step in near:
        count = count + jnp.where((t + step >= 0) & (t + step < tiles), 1, 0)
    pl.semaphore_wait(barrier, count)

    has_low, has_high = t > 0, t < tiles - 1

    low_edge = remote(
        px_in.at[pl.ds(0, 1)], px.at[c, pl.ds(rows + 1, 1)], z_send.at[0], z_recv.at[1], c, t - 1
    )
    high_edge = remote(
        px_in.at[pl.ds(rows - 1, 1)], px.at[c, pl.ds(0, 1)], z_send.at[1], z_recv.at[0], c, t + 1
    )
    pl.when(has_low)(low_edge.start)
    pl.when(has_high)(high_edge.start)

    places = (pl.ds(1, mid), pl.ds(1 + mid, rows - mid), pl.ds(0, 1), pl.ds(rows + 1, 1))
    exists = (None, None, has_low, has_high)

    def when(condition, run):
        if condition is None:
            run()
        else:
            pl.when(condition)(run)

    def own_copies(piece):
        dst = px.at[c, places[piece]]
        src = dst
        if piece == 0:
            src = px_in.at[pl.ds(0, mid)]
        if piece == 1:
            src = px_in.at[pl.ds(mid, rows - mid)]
        return [
            remote(src, dst, p_own.at[j, piece], p_recv.at[c, piece], chan, t)
            for j, chan in enumerate([partner] + peers)
        ]

    def forwards(piece):
        if piece % 2 == 0:
            ref = px.at[partner, places[piece]]
            return [
                remote(ref, ref, p_fwd_a.at[j, piece // 2], p_recv.at[partner, piece], chan, t)
                for j, chan in enumerate(peers)
            ]
        copies = []
        for j, chan in enumerate(peers):
            ref = px.at[chan, places[piece]]
            copies.append(
                remote(ref, ref, p_fwd_b.at[j, piece // 2], p_recv.at[chan, piece], partner, t)
            )
        return copies

    def forward(piece):
        def run():
            if piece % 2 == 0:
                wait_for(px.at[partner, places[piece]], p_recv.at[partner, piece])
                for copy in forwards(piece):
                    copy.start()
            else:
                for chan, copy in zip(peers, forwards(piece)):
                    wait_for(px.at[chan, places[piece]], p_recv.at[chan, piece])
                    copy.start()
        when(exists[piece], run)

    def start_own(piece):
        def run():
            for copy in own_copies(piece):
                copy.start()
        when(exists[piece], run)

    def finish_pixels():
        own_px.wait()
        for piece in range(4):
            def run(piece=piece):
                rest = corners + ([partner] if piece % 2 else peers)
                for chan in rest:
                    wait_for(px.at[chan, places[piece]], p_recv.at[chan, piece])
            when(exists[piece], run)

    def hop(kind, h, source, a):
        ref = wt.at[h, source, a]
        target = (t + 2, t - 2, sibling)[kind]
        return remote(
            ref, ref, w_send.at[kind, h, source // 2], w_recv.at[h, source, a], c, target
        )

    def send_own(kind, h):
        reach = (q < chips - 1, q > 0, None)[kind]

        def run():
            for a in range(3):
                hop(kind, h, shard, a).start()
        when(reach, run)

    def service(h, d):
        left, right = q - d, q + d
        for a in range(3):
            @pl.when((left >= 0) & (d > 0))
            def _():
                source = 2 * left + core
                wait_for(wt.at[h, source, a], w_recv.at[h, source, a])

                @pl.when(q < chips - 1)
                def _():
                    hop(RIGHT, h, source, a).start()
                hop(SIBLING, h, source, a).start()

            @pl.when((right < chips) & (d > 0))
            def _():
                source = 2 * right + core
                wait_for(wt.at[h, source, a], w_recv.at[h, source, a])

                @pl.when(q > 0)
                def _():
                    hop(LEFT, h, source, a).start()
                hop(SIBLING, h, source, a).start()
        if h + 1 < halves:
            @pl.when(left == 0)
            def _():
                send_own(RIGHT, h + 1)

            @pl.when(right == chips - 1)
            def _():
                send_own(LEFT, h + 1)

    def multiply(h, unit):
        part = acc[...]
        for a in range(3):
            window = px[unit, pl.ds(a, rows)].reshape(rows * cols, own)
            filters = wt[h, pl.ds(unit * (own // depth), own // depth), a].reshape(own, 3 * width)
            part = part + jnp.dot(window, filters, preferred_element_type=jnp.float32)
        acc[...] = part

    def compute(h, d):
        def side(s, carry):
            chip = q + d * (1 - 2 * s)
            inside = (chip >= 0) & (chip < chips) & ((s == 0) | (d > 0))

            @pl.when(inside)
            def _():
                for a in range(3):
                    source = 2 * chip + other
                    wait_for(wt.at[h, source, a], w_recv.at[h, source, a])
            mine = (d == per_unit - 1) & (s == 0)
            edge = jnp.where(s == 0, per_unit - 1, 0)
            full = (
                inside & (lax.rem(chip + per_unit, per_unit) == edge)
                & (chip // per_unit != q // per_unit)
            )

            @pl.when(mine | full)
            def _():
                multiply(h, jnp.where(mine, q // per_unit, chip // per_unit))
            return carry
        lax.fori_loop(0, 2, side, 0)

    def edges(h):
        return (
            remote(hid.at[h, pl.ds(0, 3)], hid_high.at[h], h_send.at[h, 0], h_recv.at[h, 1], c, t - 1),
            remote(hid.at[h, pl.ds(rows - 3, 3)], hid_low.at[h], h_send.at[h, 1], h_recv.at[h, 0], c, t + 1),
        )

    def activate(h):
        lanes = pl.ds(h * width, width)
        bias = conv_bias[:, lanes]
        place = lax.broadcasted_iota(jnp.int32, (cols, width), 0)

        def row(r, carry):
            base = pl.ds(pl.multiple_of(r * cols, cols), cols)
            before = pltpu.roll(acc[base, pl.ds(0, width)], 1, 0)
            after = pltpu.roll(acc[base, pl.ds(2 * width, width)], cols - 1, 0)
            value = acc[base, pl.ds(width, width)] + bias
            value = value + jnp.where(place == 0, 0.0, before)
            value = value + jnp.where(place == cols - 1, 0.0, after)
            rounded = jnp.maximum(value, 0.0).astype(jnp.bfloat16)
            hid[h, r] = rounded
            spread[3 + r, pl.ds(PAD, cols)] = rounded.astype(jnp.float32)
            return carry
        lax.fori_loop(0, rows, row, 0)
        low, high = edges(h)
        pl.when(has_low)(low.start)
        pl.when(has_high)(high.start)

    block = 32

    def taps(h, sources, first):
        lanes = pl.ds(h * width, width)

        def step(i, carry):
            base = pl.multiple_of(i * block, block)
            here = pl.ds(base, block)
            if first:
                sums = [jnp.broadcast_to(depth_bias[:, lanes], (block, width))] * rows
            else:
                sums = [total[r, here] for r in range(rows)]
            for b in range(7):
                for k in sources:
                    x = spread[k, pl.ds(base + (PAD - 3 + b), block)]
                    for r in range(rows):
                        if 0 <= k - r < 7:
                            sums[r] = sums[r] + x * depth_weight[k - r, pl.ds(b, 1), lanes]
            for r in range(rows):
                if first:
                    total[r, here] = sums[r]
                else:
                    result[h, r, here] = sums[r].astype(jnp.bfloat16)
            return carry
        lax.fori_loop(0, cols // block, step, 0)

    inner = tuple(range(3, 3 + rows))
    outer = tuple(range(3)) + tuple(range(3 + rows, 6 + rows))

    def result_copy(h):
        return pltpu.make_async_copy(
            result.at[h], out.at[:, :, pl.ds(h * width, width)], out_sem.at[h]
        )

    def last_taps(h):
        @pl.when(has_low)
        def _():
            wait_for(hid_low.at[h], h_recv.at[h, 0])
            spread[pl.ds(0, 3), pl.ds(PAD, cols)] = hid_low[h].astype(jnp.float32)

        @pl.when(has_high)
        def _():
            wait_for(hid_high.at[h], h_recv.at[h, 1])
            spread[pl.ds(3 + rows, 3), pl.ds(PAD, cols)] = hid_high[h].astype(jnp.float32)
        taps(h, outer, False)
        result_copy(h).start()

    def arrive(h):
        for load in loads[9 * h:9 * (h + 1)]:
            load.wait()

    arrive(0)
    send_own(RIGHT, 0)
    send_own(LEFT, 0)
    send_own(SIBLING, 0)
    start_own(0)
    start_own(1)
    for h in range(1, halves):
        arrive(h)
        send_own(SIBLING, h)
    service(0, 0)
    blank = jnp.zeros((units, 1, cols, own), px.dtype)

    @pl.when(t == 0)
    def _():
        px[:, pl.ds(0, 1)] = blank
        spread[pl.ds(0, 3)] = jnp.zeros((3,) + spread.shape[1:], jnp.float32)

    @pl.when(t == tiles - 1)
    def _():
        px[:, pl.ds(rows + 1, 1)] = blank
        spread[pl.ds(3 + rows, 3)] = jnp.zeros((3,) + spread.shape[1:], jnp.float32)
    spread[:, pl.ds(0, PAD)] = jnp.zeros((rows + 6, PAD, width), jnp.float32)
    spread[:, pl.ds(PAD + cols, PAD)] = jnp.zeros((rows + 6, PAD, width), jnp.float32)
    acc[...] = jnp.zeros_like(acc)

    @pl.when(has_low)
    def _():
        wait_for(px.at[c, pl.ds(0, 1)], z_recv.at[0])

    @pl.when(has_high)
    def _():
        wait_for(px.at[c, pl.ds(rows + 1, 1)], z_recv.at[1])
    start_own(2)
    start_own(3)

    def between(h, low, high):
        lax.fori_loop(low, high, lambda d, carry: (service(h, d), carry)[1], 0)

    def compute_all(h, low, high):
        lax.fori_loop(low, high, lambda d, carry: (compute(h, d), carry)[1], 0)

    service(0, 1)
    forward(0)
    forward(1)
    between(0, 2, chips - 1)
    forward(2)
    forward(3)
    service(0, chips - 1)
    for h in range(halves):
        if h + 1 < halves:
            service(h + 1, 0)
            service(h + 1, 1)
        if h == 0:
            finish_pixels()
            compute_all(h, 0, chips)
        else:
            acc[...] = jnp.zeros_like(acc)
            compute_all(h, 0, 2)
            between(h, 2, chips - 1)
            compute_all(h, 2, chips - 1)
            last_taps(h - 1)
            service(h, chips - 1)
            compute_all(h, chips - 1, chips)
        activate(h)
        taps(h, inner, True)
    last_taps(halves - 1)

    def drain(source, carry):
        for h in range(halves):
            ref = wt.at[h, 2 * source + core]

            @pl.when((q < chips - 1) & (source <= q))
            def _():
                wait_for(ref, w_send.at[RIGHT, h, source])

            @pl.when((q > 0) & (source >= q))
            def _():
                wait_for(ref, w_send.at[LEFT, h, source])
            wait_for(ref, w_send.at[SIBLING, h, source])
        return carry
    lax.fori_loop(0, chips, drain, 0)
    pl.when(has_low)(low_edge.wait_send)
    pl.when(has_high)(high_edge.wait_send)
    for piece in range(4):
        def run(piece=piece):
            for copy in own_copies(piece) + forwards(piece):
                copy.wait_send()
        when(exists[piece], run)
    for h in range(halves):
        low, high = edges(h)
        pl.when(has_low)(low.wait_send)
        pl.when(has_high)(high.wait_send)
        result_copy(h).wait()


def body(chans, tiles, pixels, conv_weight, conv_bias, depth_weight, depth_bias):
    rows, cols, own = pixels.shape
    depth = conv_weight.shape[2]
    halves = max(1, own // 128)
    width = own // halves
    chips = tiles // 2
    peers = max(1, chans // 2 - 1)
    any_space = pl.BlockSpec(memory_space=pl.ANY)
    vmem = pl.BlockSpec(memory_space=pltpu.VMEM)
    dma = pltpu.SemaphoreType.DMA
    bf16, f32 = jnp.bfloat16, jnp.float32
    return pl.pallas_call(
        functools.partial(kernel, chans, tiles),
        out_shape=jax.ShapeDtypeStruct(pixels.shape, bf16),
        in_specs=[any_space, any_space, vmem, vmem, vmem],
        out_specs=any_space,
        scratch_shapes=[
            pltpu.VMEM((chans, rows + 2, cols, own), bf16),
            pltpu.VMEM((halves, tiles, 3, depth, 3 * width), bf16),
            pltpu.VMEM((rows * cols, 3 * width), f32),
            pltpu.VMEM((halves, rows, cols, width), bf16),
            pltpu.VMEM((halves, 3, cols, width), bf16),
            pltpu.VMEM((halves, 3, cols, width), bf16),
            pltpu.VMEM((rows + 6, cols + 2 * PAD, width), f32),
            pltpu.VMEM((rows, cols, width), f32),
            pltpu.VMEM((halves, rows, cols, width), bf16),
            dma((halves + 1, 9)),
            dma((halves, tiles, 3)),
            dma((3, halves, chips)),
            dma((2,)),
            dma((2,)),
            dma((chans, 4)),
            dma((peers + 1, 4)),
            dma((peers, 2)),
            dma((peers, 2)),
            dma((halves, 2)),
            dma((halves, 2)),
            dma((halves,)),
        ],
        compiler_params=pltpu.CompilerParams(
            collective_id=0, has_side_effects=True, vmem_limit_bytes=48 * 2**20
        ),
    )(pixels, conv_weight, conv_bias.reshape(1, own), depth_weight, depth_bias.reshape(1, own))


def solution(mesh):
    in_specs = (
        P("tile", None, "chan"),
        P(None, None, "tile", "chan"),
        P("chan"),
        P(None, None, "chan"),
        P("chan"),
    )
    out_specs = P("tile", None, "chan")
    sizes = mesh.shape["chan"], mesh.shape["tile"]
    return jax.shard_map(
        functools.partial(body, *sizes), mesh=mesh, in_specs=in_specs, out_specs=out_specs,
        check_vma=False,
    )
```

time: 161 us -> 60 us (0.37)
  the two profiles are of different devices: /device:TPU:1 before, /device:TPU:19 now
where the time goes in v1:
time: 60 us; the launch traced here: 59.7 us
  Pallas kernels  55.3 us (92%)
  local copies, waits for them, and re-layouts  4.41 us (7%)
    pallas_call x1, Pallas kernels, body(): pl.pallas_call(functools.partial(kernel, chans, tiles), out_shape=jax.Sha...  55.3 us
    unnamed x11, local copies, waits for them, and re-layouts  4.41 us

profile of v1, /device:TPU:19, one launch (start us, length us, event | category | flops | bytes accessed | tf_op | source)
XLA Modules:
  0.0 59.7 jit_solution(13621327235137606507)
XLA Ops:
  0.0 0.0 copy-start.4
  0.0 0.0 copy-start.3
  0.0 0.7 %copy-done.4 = f32[256]{0:T(256)S(1)} copy-done((f32[256]{0:T(256)S(1)}, f32[256]{0:T(256)}, u32[]{:S(2)}) %copy-start.4) | copy-done | bytes 1048
  0.7 0.0 copy-done.3
  0.7 0.0 copy-start
  0.7 1.1 %copy-done = bf16[3,3,128,256]{3,2,1,0:T(8,128)(2,1)S(1)} copy-done((bf16[3,3,128,256]{3,2,1,0:T(8,128)(2,1)S(1)}, bf16[3,3,128,256]{3,2,1,0:T(8,128)(2,1)}, u32[]{:S(2)}) %copy-start) | copy-done | bytes 589848
  1.8 0.0 copy-start.1
  1.8 1.0 %copy-done.1 = bf16[4,256,256]{2,1,0:T(8,128)(2,1)S(1)} copy-done((bf16[4,256,256]{2,1,0:T(8,128)(2,1)S(1)}, bf16[4,256,256]{2,1,0:T(8,128)(2,1)}, u32[]{:S(2)}) %copy-start.1) | copy-done | bytes 524312
  2.8 0.0 copy-start.2
  2.8 0.8 %copy-done.2 = f32[7,7,256]{2,1,0:T(8,128)S(1)} copy-done((f32[7,7,256]{2,1,0:T(8,128)S(1)}, f32[7,7,256]{2,1,0:T(8,128)}, u32[]{:S(2)}) %copy-start.2) | copy-done | bytes 50200
  3.6 55.3 %shard_map.55 = bf16[4,256,256]{2,1,0:T(8,128)(2,1)S(1)} custom-call(bf16[4,256,256]{2,1,0:T(8,128)(2,1)S(1)} %copy-done.1, bf16[3,3,128,256]{3,2,1,0:T(8,128)(2,1)S(1)} %copy-done, f32[1,256]{1,0:T(1,128)S(1)} %bitcast.2, f32[7,7,256]{2,1,0:T(8,128)S(1)} %copy-done.2, f32[1,256]{1,0:T(1,128)S(1)} %bitcast.3), custom_call_target="tpu_custom_call" | custom-call | tf_op jit(solution)/shard_map/pallas_call | solution.py:415
  58.9 0.8 %copy.7 = bf16[4,256,256]{2,1,0:T(8,128)(2,1)} copy(bf16[4,256,256]{2,1,0:T(8,128)(2,1)S(1)} %shard_map.55) | data formatting | bytes 1048576
Async XLA Ops:
  0.0 0.7 %copy-start.4 = (f32[256]{0:T(256)S(1)}, f32[256]{0:T(256)}, u32[]{:S(2)}) copy-start(f32[256]{0:T(256)} %param.9) | copy-start | bytes 3076
  0.0 0.7 %copy-start.3 = (f32[256]{0:T(256)S(1)}, f32[256]{0:T(256)}, u32[]{:S(2)}) copy-start(f32[256]{0:T(256)} %param.7) | copy-start | bytes 3076
  0.7 1.1 %copy-start = (bf16[3,3,128,256]{3,2,1,0:T(8,128)(2,1)S(1)}, bf16[3,3,128,256]{3,2,1,0:T(8,128)(2,1)}, u32[]{:S(2)}) copy-start(bf16[3,3,128,256]{3,2,1,0:T(8,128)(2,1)} %w_in.1) | copy-start | bytes 1769476
  1.8 1.0 %copy-start.1 = (bf16[4,256,256]{2,1,0:T(8,128)(2,1)S(1)}, bf16[4,256,256]{2,1,0:T(8,128)(2,1)}, u32[]{:S(2)}) copy-start(bf16[4,256,256]{2,1,0:T(8,128)(2,1)} %px_in.1) | copy-start | bytes 1572868
  2.8 0.8 %copy-start.2 = (f32[7,7,256]{2,1,0:T(8,128)S(1)}, f32[7,7,256]{2,1,0:T(8,128)}, u32[]{:S(2)}) copy-start(f32[7,7,256]{2,1,0:T(8,128)} %depth_weight.1) | copy-start | bytes 150532

commit v2 on v1

--- a/solution.py
+++ b/solution.py
@@ -12,10 +12,10 @@
 
 
 def kernel(
-    chans, tiles, px_in, w_in, conv_bias, depth_weight, depth_bias, out,
-    px, wt, acc, hid, hid_low, hid_high, spread, total, result,
+    chans, tiles, px_in, w_in, conv_bias_in, depth_weight_in, depth_bias_in, out,
+    conv_bias, depth_weight, depth_bias, px, wt, acc, hid, hid_low, hid_high, spread, total, result,
     load_sem, w_recv, w_send, z_send, z_recv, p_recv, p_own, p_fwd_a, p_fwd_b,
-    h_send, h_recv, out_sem,
+    h_send, h_recv, out_sem, small_sem,
 ):
     rows, cols, own = px_in.shape
     halves, _, _, depth, _ = wt.shape
@@ -50,6 +50,13 @@
             barrier, inc=1, device_id=(chan, tile), device_id_type=pl.DeviceIdType.MESH
         )
 
+    near = (-2, -1, 1, 2)
+    for step in near:
+        @pl.when((t + step >= 0) & (t + step < tiles))
+        def _():
+            tell(c, t + step)
+    for chan in [partner] + peers:
+        tell(chan, t)
     shard = 2 * q + core
     loads = []
     for h in range(halves):
@@ -64,14 +71,15 @@
     for load in loads:
         load.start()
     own_px.start()
-
-    near = (-2, -1, 1, 2)
-    for step in near:
-        @pl.when((t + step >= 0) & (t + step < tiles))
-        def _():
-            tell(c, t + step)
-    for chan in [partner] + peers:
-        tell(chan, t)
+    smalls = [
+        pltpu.make_async_copy(src, dst, small_sem.at[i])
+        for i, (src, dst) in enumerate((
+            (conv_bias_in, conv_bias), (depth_weight_in, depth_weight), (depth_bias_in, depth_bias),
+        ))
+    ]
+    for small in smalls:
+        small.start()
+
     count = high_count
     for step in near:
         count = count + jnp.where((t + step >= 0) & (t + step < tiles), 1, 0)
@@ -166,28 +174,33 @@
                 hop(kind, h, shard, a).start()
         when(reach, run)
 
+    def service_piece(h, d, a):
+        left, right = q - d, q + d
+
+        @pl.when((left >= 0) & (d > 0))
+        def _():
+            source = 2 * left + core
+            wait_for(wt.at[h, source, a], w_recv.at[h, source, a])
+
+            @pl.when(q < chips - 1)
+            def _():
+                hop(RIGHT, h, source, a).start()
+            hop(SIBLING, h, source, a).start()
+
+        @pl.when((right < chips) & (d > 0))
+        def _():
+            source = 2 * right + core
+            wait_for(wt.at[h, source, a], w_recv.at[h, source, a])
+
+            @pl.when(q > 0)
+            def _():
+                hop(LEFT, h, source, a).start()
+            hop(SIBLING, h, source, a).start()
+
     def service(h, d):
         left, right = q - d, q + d
         for a in range(3):
-            @pl.when((left >= 0) & (d > 0))
-            def _():
-                source = 2 * left + core
-                wait_for(wt.at[h, source, a], w_recv.at[h, source, a])
-
-                @pl.when(q < chips - 1)
-                def _():
-                    hop(RIGHT, h, source, a).start()
-                hop(SIBLING, h, source, a).start()
-
-            @pl.when((right < chips) & (d > 0))
-            def _():
-                source = 2 * right + core
-                wait_for(wt.at[h, source, a], w_recv.at[h, source, a])
-
-                @pl.when(q > 0)
-                def _():
-                    hop(LEFT, h, source, a).start()
-                hop(SIBLING, h, source, a).start()
+            service_piece(h, d, a)
         if h + 1 < halves:
             @pl.when(left == 0)
             def _():
@@ -197,13 +210,29 @@
             def _():
                 send_own(LEFT, h + 1)
 
-    def multiply(h, unit):
+    def multiply(h, unit, taps=(0, 1, 2)):
         part = acc[...]
-        for a in range(3):
+        for a in taps:
             window = px[unit, pl.ds(a, rows)].reshape(rows * cols, own)
             filters = wt[h, pl.ds(unit * (own // depth), own // depth), a].reshape(own, 3 * width)
             part = part + jnp.dot(window, filters, preferred_element_type=jnp.float32)
         acc[...] = part
+
+    def last_step(h):
+        d = chips - 1
+        if per_unit > 1:
+            service(h, d)
+            compute(h, d)
+            return
+        for a in range(3):
+            service_piece(h, d, a)
+
+            @pl.when((q == 0) | (q == d))
+            def _():
+                unit = jnp.where(q == 0, d, 0)
+                source = 2 * unit + other
+                wait_for(wt.at[h, source, a], w_recv.at[h, source, a])
+                multiply(h, unit, (a,))
 
     def compute(h, d):
         def side(s, carry):
@@ -248,12 +277,30 @@
             value = value + jnp.where(place == cols - 1, 0.0, after)
             rounded = jnp.maximum(value, 0.0).astype(jnp.bfloat16)
             hid[h, r] = rounded
-            spread[3 + r, pl.ds(PAD, cols)] = rounded.astype(jnp.float32)
+            spread[h, 3 + r, pl.ds(PAD, cols)] = rounded.astype(jnp.float32)
             return carry
         lax.fori_loop(0, rows, row, 0)
         low, high = edges(h)
-        pl.when(has_low)(low.start)
-        pl.when(has_high)(high.start)
+        pl.when(has_low & low_free)(low.start)
+        pl.when(has_high & high_free)(high.start)
+
+    low_free = (core == 1) | (q == chips - 1)
+    high_free = (core == 0) | (q == 0)
+
+    def last_out(kind, condition):
+        source = (0, chips - 1)[kind]
+
+        @pl.when(condition)
+        def _():
+            wait_for(wt.at[halves - 1, 2 * source + core], w_send.at[kind, halves - 1, source])
+
+    def release():
+        last_out(LEFT, q > 0)
+        last_out(RIGHT, q < chips - 1)
+        for h in range(halves):
+            low, high = edges(h)
+            pl.when(has_low & jnp.logical_not(low_free))(low.start)
+            pl.when(has_high & jnp.logical_not(high_free))(high.start)
 
     block = 32
 
@@ -266,16 +313,16 @@
             if first:
                 sums = [jnp.broadcast_to(depth_bias[:, lanes], (block, width))] * rows
             else:
-                sums = [total[r, here] for r in range(rows)]
+                sums = [total[h, r, here] for r in range(rows)]
             for b in range(7):
                 for k in sources:
-                    x = spread[k, pl.ds(base + (PAD - 3 + b), block)]
+                    x = spread[h, k, pl.ds(base + (PAD - 3 + b), block)]
                     for r in range(rows):
                         if 0 <= k - r < 7:
                             sums[r] = sums[r] + x * depth_weight[k - r, pl.ds(b, 1), lanes]
             for r in range(rows):
                 if first:
-                    total[r, here] = sums[r]
+                    total[h, r, here] = sums[r]
                 else:
                     result[h, r, here] = sums[r].astype(jnp.bfloat16)
             return carry
@@ -293,12 +340,12 @@
         @pl.when(has_low)
         def _():
             wait_for(hid_low.at[h], h_recv.at[h, 0])
-            spread[pl.ds(0, 3), pl.ds(PAD, cols)] = hid_low[h].astype(jnp.float32)
+            spread[h, pl.ds(0, 3), pl.ds(PAD, cols)] = hid_low[h].astype(jnp.float32)
 
         @pl.when(has_high)
         def _():
             wait_for(hid_high.at[h], h_recv.at[h, 1])
-            spread[pl.ds(3 + rows, 3), pl.ds(PAD, cols)] = hid_high[h].astype(jnp.float32)
+            spread[h, pl.ds(3 + rows, 3), pl.ds(PAD, cols)] = hid_high[h].astype(jnp.float32)
         taps(h, outer, False)
         result_copy(h).start()
 
@@ -321,14 +368,14 @@
     @pl.when(t == 0)
     def _():
         px[:, pl.ds(0, 1)] = blank
-        spread[pl.ds(0, 3)] = jnp.zeros((3,) + spread.shape[1:], jnp.float32)
+        spread[:, pl.ds(0, 3)] = jnp.zeros((halves, 3) + spread.shape[2:], jnp.float32)
 
     @pl.when(t == tiles - 1)
     def _():
         px[:, pl.ds(rows + 1, 1)] = blank
-        spread[pl.ds(3 + rows, 3)] = jnp.zeros((3,) + spread.shape[1:], jnp.float32)
-    spread[:, pl.ds(0, PAD)] = jnp.zeros((rows + 6, PAD, width), jnp.float32)
-    spread[:, pl.ds(PAD + cols, PAD)] = jnp.zeros((rows + 6, PAD, width), jnp.float32)
+        spread[:, pl.ds(3 + rows, 3)] = jnp.zeros((halves, 3) + spread.shape[2:], jnp.float32)
+    spread[:, :, pl.ds(0, PAD)] = jnp.zeros((halves, rows + 6, PAD, width), jnp.float32)
+    spread[:, :, pl.ds(PAD + cols, PAD)] = jnp.zeros((halves, rows + 6, PAD, width), jnp.float32)
     acc[...] = jnp.zeros_like(acc)
 
     @pl.when(has_low)
@@ -366,22 +413,29 @@
             compute_all(h, 0, 2)
             between(h, 2, chips - 1)
             compute_all(h, 2, chips - 1)
-            last_taps(h - 1)
-            service(h, chips - 1)
-            compute_all(h, chips - 1, chips)
+            last_step(h)
+        if h == 0:
+            for small in smalls:
+                small.wait()
         activate(h)
         taps(h, inner, True)
-    last_taps(halves - 1)
+    release()
+    for h in range(halves):
+        last_taps(h)
 
     def drain(source, carry):
         for h in range(halves):
             ref = wt.at[h, 2 * source + core]
 
-            @pl.when((q < chips - 1) & (source <= q))
+            kept = True if h < halves - 1 else source != 0
+
+            @pl.when((q < chips - 1) & (source <= q) & kept)
             def _():
                 wait_for(ref, w_send.at[RIGHT, h, source])
 
-            @pl.when((q > 0) & (source >= q))
+            kept = True if h < halves - 1 else source != chips - 1
+
+            @pl.when((q > 0) & (source >= q) & kept)
             def _():
                 wait_for(ref, w_send.at[LEFT, h, source])
             wait_for(ref, w_send.at[SIBLING, h, source])
@@ -409,23 +463,25 @@
     chips = tiles // 2
     peers = max(1, chans // 2 - 1)
     any_space = pl.BlockSpec(memory_space=pl.ANY)
-    vmem = pl.BlockSpec(memory_space=pltpu.VMEM)
     dma = pltpu.SemaphoreType.DMA
     bf16, f32 = jnp.bfloat16, jnp.float32
     return pl.pallas_call(
         functools.partial(kernel, chans, tiles),
         out_shape=jax.ShapeDtypeStruct(pixels.shape, bf16),
-        in_specs=[any_space, any_space, vmem, vmem, vmem],
+        in_specs=[any_space] * 5,
         out_specs=any_space,
         scratch_shapes=[
+            pltpu.VMEM((1, own), f32),
+            pltpu.VMEM(depth_weight.shape, f32),
+            pltpu.VMEM((1, own), f32),
             pltpu.VMEM((chans, rows + 2, cols, own), bf16),
             pltpu.VMEM((halves, tiles, 3, depth, 3 * width), bf16),
             pltpu.VMEM((rows * cols, 3 * width), f32),
             pltpu.VMEM((halves, rows, cols, width), bf16),
             pltpu.VMEM((halves, 3, cols, width), bf16),
             pltpu.VMEM((halves, 3, cols, width), bf16),
-            pltpu.VMEM((rows + 6, cols + 2 * PAD, width), f32),
-            pltpu.VMEM((rows, cols, width), f32),
+            pltpu.VMEM((halves, rows + 6, cols + 2 * PAD, width), f32),
+            pltpu.VMEM((halves, rows, cols, width), f32),
             pltpu.VMEM((halves, rows, cols, width), bf16),
             dma((halves + 1, 9)),
             dma((halves, tiles, 3)),
@@ -439,9 +495,10 @@
             dma((halves, 2)),
             dma((halves, 2)),
             dma((halves,)),
+            dma((3,)),
         ],
         compiler_params=pltpu.CompilerParams(
-            collective_id=0, has_side_effects=True, vmem_limit_bytes=48 * 2**20
+            collective_id=0, has_side_effects=True, vmem_limit_bytes=62 * 2**20
         ),
     )(pixels, conv_weight, conv_bias.reshape(1, own), depth_weight, depth_bias.reshape(1, own))
 

time: 60 us -> 58.8 us (0.980)
  the two profiles are of different devices: /device:TPU:19 before, /device:TPU:1 now
where the time goes in v2:
time: 58.8 us; the launch traced here: 58.3 us
  Pallas kernels  56.5 us (96%)
  local copies, waits for them, and re-layouts  1.87 us (3%)
    pallas_call x1, Pallas kernels, body(): pl.pallas_call(functools.partial(kernel, chans, tiles), out_shape=jax.Sha...  56.5 us
    unnamed x1, local copies, waits for them, and re-layouts  1.87 us

profile of v2, /device:TPU:1, one launch (start us, length us, event | category | flops | bytes accessed | tf_op | source)
XLA Modules:
  0.0 58.3 jit_solution(20506817705676431)
XLA Ops:
  0.0 56.5 %shard_map.55 = bf16[4,256,256]{2,1,0:T(8,128)(2,1)} custom-call(bf16[4,256,256]{2,1,0:T(8,128)(2,1)} %px_in.1, bf16[3,3,128,256]{3,2,1,0:T(8,128)(2,1)} %w_in.1, f32[1,256]{1,0:T(1,128)} %bitcast.2, f32[7,7,256]{2,1,0:T(8,128)} %depth_weight_in.1, f32[1,256]{1,0:T(1,128)} %bitcast.3), custom_call_target="tpu_custom_call" | custom-call | tf_op jit(solution)/shard_map/pallas_call | solution.py:468
  56.5 1.9 %copy.7 = bf16[4,256,256]{2,1,0:T(8,128)(2,1)} copy(bf16[4,256,256]{2,1,0:T(8,128)(2,1)} %shard_map.55) | data formatting | bytes 1048576

commit v3 on v2

--- a/solution.py
+++ b/solution.py
@@ -304,7 +304,7 @@
 
     block = 32
 
-    def taps(h, sources, first):
+    def taps(h, sources, first, final):
         lanes = pl.ds(h * width, width)
 
         def step(i, carry):
@@ -321,32 +321,51 @@
                         if 0 <= k - r < 7:
                             sums[r] = sums[r] + x * depth_weight[k - r, pl.ds(b, 1), lanes]
             for r in range(rows):
-                if first:
+                if final:
+                    result[h, r, here] = sums[r].astype(jnp.bfloat16)
+                else:
                     total[h, r, here] = sums[r]
-                else:
-                    result[h, r, here] = sums[r].astype(jnp.bfloat16)
             return carry
         lax.fori_loop(0, cols // block, step, 0)
 
     inner = tuple(range(3, 3 + rows))
-    outer = tuple(range(3)) + tuple(range(3 + rows, 6 + rows))
+    lower = tuple(range(3))
+    upper = tuple(range(3 + rows, 6 + rows))
 
     def result_copy(h):
         return pltpu.make_async_copy(
             result.at[h], out.at[:, :, pl.ds(h * width, width)], out_sem.at[h]
         )
 
-    def last_taps(h):
-        @pl.when(has_low)
-        def _():
-            wait_for(hid_low.at[h], h_recv.at[h, 0])
-            spread[h, pl.ds(0, 3), pl.ds(PAD, cols)] = hid_low[h].astype(jnp.float32)
-
-        @pl.when(has_high)
-        def _():
-            wait_for(hid_high.at[h], h_recv.at[h, 1])
-            spread[h, pl.ds(3 + rows, 3), pl.ds(PAD, cols)] = hid_high[h].astype(jnp.float32)
-        taps(h, outer, False)
+    def take_low(h):
+        wait_for(hid_low.at[h], h_recv.at[h, 0])
+        spread[h, pl.ds(0, 3), pl.ds(PAD, cols)] = hid_low[h].astype(jnp.float32)
+
+    def take_high(h):
+        wait_for(hid_high.at[h], h_recv.at[h, 1])
+        spread[h, pl.ds(3 + rows, 3), pl.ds(PAD, cols)] = hid_high[h].astype(jnp.float32)
+
+    def near_taps(h):
+        @pl.when(core == 0)
+        def _():
+            take_high(h)
+            taps(h, upper, False, False)
+
+        @pl.when(core == 1)
+        def _():
+            take_low(h)
+            taps(h, lower, False, False)
+
+    def far_taps(h):
+        @pl.when(core == 0)
+        def _():
+            pl.when(has_low)(functools.partial(take_low, h))
+            taps(h, lower, False, True)
+
+        @pl.when(core == 1)
+        def _():
+            pl.when(has_high)(functools.partial(take_high, h))
+            taps(h, upper, False, True)
         result_copy(h).start()
 
     def arrive(h):
@@ -413,15 +432,15 @@
             compute_all(h, 0, 2)
             between(h, 2, chips - 1)
             compute_all(h, 2, chips - 1)
+            near_taps(h - 1)
             last_step(h)
         if h == 0:
             for small in smalls:
                 small.wait()
         activate(h)
-        taps(h, inner, True)
+        taps(h, inner, True, False)
+    near_taps(halves - 1)
     release()
-    for h in range(halves):
-        last_taps(h)
 
     def drain(source, carry):
         for h in range(halves):
@@ -448,6 +467,8 @@
             for copy in own_copies(piece) + forwards(piece):
                 copy.wait_send()
         when(exists[piece], run)
+    for h in range(halves):
+        far_taps(h)
     for h in range(halves):
         low, high = edges(h)
         pl.when(has_low)(low.wait_send)
@@ -468,7 +489,7 @@
     return pl.pallas_call(
         functools.partial(kernel, chans, tiles),
         out_shape=jax.ShapeDtypeStruct(pixels.shape, bf16),
-        in_specs=[any_space] * 5,
+        in_specs=[pl.BlockSpec(memory_space=pltpu.HBM)] * 5,
         out_specs=any_space,
         scratch_shapes=[
             pltpu.VMEM((1, own), f32),
@@ -498,9 +519,14 @@
             dma((3,)),
         ],
         compiler_params=pltpu.CompilerParams(
-            collective_id=0, has_side_effects=True, vmem_limit_bytes=62 * 2**20
+            collective_id=0, has_side_effects=True, vmem_limit_bytes=40 * 2**20
         ),
-    )(pixels, conv_weight, conv_bias.reshape(1, own), depth_weight, depth_bias.reshape(1, own))
+    )(*(
+        pltpu.with_memory_space_constraint(x, pltpu.HBM)
+        for x in (
+            pixels, conv_weight, conv_bias.reshape(1, own), depth_weight, depth_bias.reshape(1, own)
+        )
+    ))
 
 
 def solution(mesh):

time: 58.8 us -> 56.7 us (0.964)
  Pallas kernels: 56.5 us -> 55.1 us
  local copies, waits for them, and re-layouts: 1.87 us -> 0.8 us
    pallas_call x1, Pallas kernels: 56.5 us -> 55.1 us  [body(): pl.pallas_call(functools.partial(kernel, chans, tiles), out_shape=jax.Sha...]
    unnamed x1, local copies, waits for them, and re-layouts: 1.87 us -> 0.8 us
where the time goes in v3:
time: 56.7 us; the launch traced here: 55.9 us
  Pallas kernels  55.1 us (97%)
  local copies, waits for them, and re-layouts  0.8 us (1%)
    pallas_call x1, Pallas kernels, body(): pl.pallas_call(functools.partial(kernel, chans, tiles), out_shape=jax.Sha...  55.1 us

profile of v3, /device:TPU:1, one launch (start us, length us, event | category | flops | bytes accessed | tf_op | source)
XLA Modules:
  0.0 55.9 jit_solution(265168328119452697)
XLA Ops:
  0.0 55.1 %shard_map.55 = bf16[4,256,256]{2,1,0:T(8,128)(2,1)S(1)} custom-call(bf16[4,256,256]{2,1,0:T(8,128)(2,1)} %px_in.1, bf16[3,3,128,256]{3,2,1,0:T(8,128)(2,1)} %w_in.1, f32[1,256]{1,0:T(1,128)} %bitcast.2, f32[7,7,256]{2,1,0:T(8,128)} %depth_weight_in.1, f32[1,256]{1,0:T(1,128)} %bitcast.3), custom_call_target="tpu_custom_call" | custom-call | tf_op jit(solution)/shard_map/pallas_call | solution.py:489
  55.2 0.8 %copy.7 = bf16[4,256,256]{2,1,0:T(8,128)(2,1)} copy(bf16[4,256,256]{2,1,0:T(8,128)(2,1)S(1)} %shard_map.55) | data formatting | bytes 1048576

commit v4 on v3

--- a/solution.py
+++ b/solution.py
@@ -420,18 +420,19 @@
     forward(2)
     forward(3)
     service(0, chips - 1)
+    early = jnp.where((q > 0) & (q < chips - 1), chips - 1, 2)
     for h in range(halves):
         if h + 1 < halves:
             service(h + 1, 0)
             service(h + 1, 1)
+            between(h + 1, 2, early)
         if h == 0:
             finish_pixels()
             compute_all(h, 0, chips)
         else:
             acc[...] = jnp.zeros_like(acc)
-            compute_all(h, 0, 2)
-            between(h, 2, chips - 1)
-            compute_all(h, 2, chips - 1)
+            between(h, early, chips - 1)
+            compute_all(h, 0, chips - 1)
             near_taps(h - 1)
             last_step(h)
         if h == 0:

time: 56.7 us -> 55 us (0.970); the launches traced: 55.9 us -> 54.9 us
  Pallas kernels: 55.1 us -> 54.1 us
    pallas_call x1, Pallas kernels: 55.1 us -> 54.1 us  [body(): pl.pallas_call(functools.partial(kernel, chans, tiles), out_shape=jax.Sha...]
where the time goes in v4:
time: 55 us; the launch traced here: 54.9 us
  Pallas kernels  54.1 us (98%)
  local copies, waits for them, and re-layouts  0.8 us (1%)
    pallas_call x1, Pallas kernels, body(): pl.pallas_call(functools.partial(kernel, chans, tiles), out_shape=jax.Sha...  54.1 us

profile of v4, /device:TPU:1, one launch (start us, length us, event | category | flops | bytes accessed | tf_op | source)
XLA Modules:
  0.0 54.9 jit_solution(79329971241440498)
XLA Ops:
  0.0 54.1 %shard_map.55 = bf16[4,256,256]{2,1,0:T(8,128)(2,1)S(1)} custom-call(bf16[4,256,256]{2,1,0:T(8,128)(2,1)} %px_in.1, bf16[3,3,128,256]{3,2,1,0:T(8,128)(2,1)} %w_in.1, f32[1,256]{1,0:T(1,128)} %bitcast.2, f32[7,7,256]{2,1,0:T(8,128)} %depth_weight_in.1, f32[1,256]{1,0:T(1,128)} %bitcast.3), custom_call_target="tpu_custom_call" | custom-call | tf_op jit(solution)/shard_map/pallas_call | solution.py:490
  54.1 0.8 %copy.7 = bf16[4,256,256]{2,1,0:T(8,128)(2,1)} copy(bf16[4,256,256]{2,1,0:T(8,128)(2,1)S(1)} %shard_map.55) | data formatting | bytes 1048576

commit v5 on v4

--- a/solution.py
+++ b/solution.py
@@ -295,8 +295,8 @@
             wait_for(wt.at[halves - 1, 2 * source + core], w_send.at[kind, halves - 1, source])
 
     def release():
-        last_out(LEFT, q > 0)
-        last_out(RIGHT, q < chips - 1)
+        last_out(LEFT, (q > 0) & (core == 0))
+        last_out(RIGHT, (q < chips - 1) & (core == 1))
         for h in range(halves):
             low, high = edges(h)
             pl.when(has_low & jnp.logical_not(low_free))(low.start)
@@ -447,13 +447,13 @@
         for h in range(halves):
             ref = wt.at[h, 2 * source + core]
 
-            kept = True if h < halves - 1 else source != 0
+            kept = True if h < halves - 1 else (source != 0) | (core == 0)
 
             @pl.when((q < chips - 1) & (source <= q) & kept)
             def _():
                 wait_for(ref, w_send.at[RIGHT, h, source])
 
-            kept = True if h < halves - 1 else source != chips - 1
+            kept = True if h < halves - 1 else (source != chips - 1) | (core == 1)
 
             @pl.when((q > 0) & (source >= q) & kept)
             def _():

time: 55 us -> 55 us (level)
  no operation moved by 1% of the time
where the time goes in v5:
time: 55 us; the launch traced here: 54.9 us
  Pallas kernels  54.1 us (98%)
  local copies, waits for them, and re-layouts  0.8 us (1%)
    pallas_call x1, Pallas kernels, body(): pl.pallas_call(functools.partial(kernel, chans, tiles), out_shape=jax.Sha...  54.1 us

profile of v5, /device:TPU:1, one launch (start us, length us, event | category | flops | bytes accessed | tf_op | source)
XLA Modules:
  0.0 54.9 jit_solution(10073624199069442069)
XLA Ops:
  0.0 54.1 %shard_map.55 = bf16[4,256,256]{2,1,0:T(8,128)(2,1)S(1)} custom-call(bf16[4,256,256]{2,1,0:T(8,128)(2,1)} %px_in.1, bf16[3,3,128,256]{3,2,1,0:T(8,128)(2,1)} %w_in.1, f32[1,256]{1,0:T(1,128)} %bitcast.2, f32[7,7,256]{2,1,0:T(8,128)} %depth_weight_in.1, f32[1,256]{1,0:T(1,128)} %bitcast.3), custom_call_target="tpu_custom_call" | custom-call | tf_op jit(solution)/shard_map/pallas_call | solution.py:490
  54.1 0.8 %copy.7 = bf16[4,256,256]{2,1,0:T(8,128)(2,1)} copy(bf16[4,256,256]{2,1,0:T(8,128)(2,1)S(1)} %shard_map.55) | data formatting | bytes 1048576
